TPU v7x, 256 devices: a whole 4x4x8 slice. The times are simulated.
256 devices in a mesh: dp: 8 (over z_hi, y), seq: 32 (over z_lo, x, core).
Axes of the slice: x: 4, y: 4, z: 8 (z_hi: 2, z_lo: 4; z = z_hi * 4 + z_lo), core: 2. Of those that a mesh axis runs over, the one named last changes fastest.
Arguments:
- video: bfloat16 [8, 32, 256, 768], P('dp', 'seq'), may hold values from -6 to 6
- w_qkv_space: bfloat16 [768, 2304], replicated, may hold values from -5.809587 to 5.809587
- w_out_space: bfloat16 [768, 768], replicated, may hold values from -0.21875 to 0.21875
- w_qkv_time: bfloat16 [768, 2304], replicated, may hold values from -5.809587 to 5.809587
- w_out_time: bfloat16 [768, 768], replicated, may hold values from -0.21875 to 0.21875
- grad_out: bfloat16 [8, 32, 256, 768], P('dp', 'seq'), may hold values from -24 to 24
Outputs:
- out_video: bfloat16 [8, 32, 256, 768], P('dp', 'seq')
- grad_video: bfloat16 [8, 32, 256, 768], P('dp', 'seq')
- grad_qkv_space: float32 [768, 2304], P('seq')
- grad_out_space: float32 [768, 768], P('seq')
- grad_qkv_time: float32 [768, 2304], P('seq')
- grad_out_time: float32 [768, 768], P('seq')
All inputs are finite; a program needn't handle non-finite values.
Results may differ from a plain program's by a relative error of at most 0.038.
Values may be sent and summed in bfloat16 or wider, within the bound.
A program may use at most 128 MiB of HBM per device.

v0:
```python
import math

import jax
import jax.numpy as jnp
from jax import lax
from jax.sharding import PartitionSpec as P

HD = 64


epsilon = 1e-05


def forms(time_major):
    if time_major:
        return ("lbhd", "mbhd")
    return ("blhd", "bmhd")


def normalize(rows_wide):
    centre_mean = jnp.mean(rows_wide, axis=-1, keepdims=True)
    centred = rows_wide - centre_mean
    variance = jnp.mean(centred * centred, axis=-1, keepdims=True)
    inverse = lax.rsqrt(variance + epsilon)
    return (centred * inverse, inverse)


def attend(queries, keys_in, values, time_major):
    query_form, key_form = forms(time_major)
    factor = 1.0 / math.sqrt(HD)
    scores = (
        jnp.einsum(
            query_form + "," + key_form + "->bhlm",
            queries.astype(jnp.float32),
            keys_in.astype(jnp.float32),
        )
        * factor
    )
    highest = jnp.max(scores, axis=-1, keepdims=True)
    weights = jnp.exp(scores - highest)
    probs_full = weights / jnp.sum(weights, axis=-1, keepdims=True)
    probs_low = lax.optimization_barrier(probs_full.astype(jnp.bfloat16))
    attended = jnp.einsum(
        "bhlm," + key_form + "->" + query_form,
        probs_low.astype(jnp.float32),
        values.astype(jnp.float32),
    )
    return (attended.astype(jnp.bfloat16), probs_full, probs_low)


def attend_back(queries, keys_in, values, probs_full, probs_low, d_attended, time_major):
    query_form, key_form = forms(time_major)
    factor = 1.0 / math.sqrt(HD)
    d_wide = d_attended.astype(jnp.float32)
    d_values = jnp.einsum(
        "bhlm," + query_form + "->" + key_form, probs_low.astype(jnp.float32), d_wide
    )
    d_probs = jnp.einsum(query_form + "," + key_form + "->bhlm", d_wide, values.astype(jnp.float32))
    d_scores = (
        probs_full * (d_probs - jnp.sum(d_probs * probs_full, axis=-1, keepdims=True)) * factor
    )
    d_queries = jnp.einsum(
        "bhlm," + key_form + "->" + query_form, d_scores, keys_in.astype(jnp.float32)
    )
    d_keys = jnp.einsum(
        "bhlm," + query_form + "->" + key_form, d_scores, queries.astype(jnp.float32)
    )
    return (
        d_queries.astype(jnp.bfloat16),
        d_keys.astype(jnp.bfloat16),
        d_values.astype(jnp.bfloat16),
    )


def block_forward(tokens_in, w_qkv, w_out, time_major):
    dim_one, dim_two, feature_count = tokens_in.shape
    head_count = w_out.shape[0] // HD
    rows_wide = tokens_in.reshape(-1, feature_count).astype(jnp.float32)
    normed, _ = normalize(rows_wide)
    normed_low = normed.astype(jnp.bfloat16)
    projected = jnp.dot(normed_low, w_qkv, preferred_element_type=jnp.float32).astype(jnp.bfloat16)
    pieces = projected.reshape(dim_one, dim_two, 3, head_count, HD)
    queries = pieces[:, :, 0]
    keys_in = pieces[:, :, 1]
    values = pieces[:, :, 2]
    attended, probs_full, probs_low = attend(queries, keys_in, values, time_major)
    attended_rows = attended.reshape(-1, w_out.shape[0])
    summed = rows_wide + jnp.dot(attended_rows, w_out, preferred_element_type=jnp.float32)
    output_rows = summed.astype(jnp.bfloat16).reshape(tokens_in.shape)
    return (
        output_rows,
        (normed_low, queries, keys_in, values, probs_full, probs_low, attended_rows),
    )


def block_backward(tokens_in, saved, grad_rows, w_qkv, w_out, time_major):
    normed_low, queries, keys_in, values, probs_full, probs_low, attended_rows = saved
    dim_one, dim_two, feature_count = tokens_in.shape
    inner_width = w_out.shape[0]
    head_count = inner_width // HD
    grad_flat = grad_rows.reshape(-1, feature_count)
    grad_wout = jnp.dot(attended_rows.T, grad_flat, preferred_element_type=jnp.float32)
    d_attended = jnp.dot(grad_flat, w_out.T, preferred_element_type=jnp.float32).astype(
        jnp.bfloat16
    )
    d_attended = d_attended.reshape(dim_one, dim_two, head_count, HD)
    d_queries, d_keys, d_values = attend_back(
        queries, keys_in, values, probs_full, probs_low, d_attended, time_major
    )
    d_projected = jnp.stack([d_queries, d_keys, d_values], axis=2).reshape(-1, 3 * inner_width)
    grad_wqkv = jnp.dot(normed_low.T, d_projected, preferred_element_type=jnp.float32)
    d_normed = jnp.dot(d_projected, w_qkv.T, preferred_element_type=jnp.float32)
    rows_wide = tokens_in.reshape(-1, feature_count).astype(jnp.float32)
    normed, inverse = normalize(rows_wide)
    d_centre = jnp.mean(d_normed, axis=-1, keepdims=True)
    d_spread = jnp.mean(d_normed * normed, axis=-1, keepdims=True)
    d_rows = inverse * (d_normed - d_centre - normed * d_spread)
    d_input = (grad_flat.astype(jnp.float32) + d_rows).astype(jnp.bfloat16).reshape(tokens_in.shape)
    return (d_input, grad_wqkv, grad_wout)


def shards(video, w_qkv_space, w_out_space, w_qkv_time, w_out_time, grad_out):
    frames_here = video[0]
    group_size = lax.axis_size("seq")
    frames_dev, patch_total, feature_count = frames_here.shape
    patch_share = patch_total // group_size
    space_out, space_saved = block_forward(frames_here, w_qkv_space, w_out_space, False)
    space_parts = space_out.reshape(frames_dev, group_size, patch_share, feature_count)
    grad_parts = grad_out[0].reshape(frames_dev, group_size, patch_share, feature_count)
    arrived = lax.all_to_all(space_parts, "seq", split_axis=1, concat_axis=0, tiled=True)
    time_in = arrived[:, 0]
    time_out, time_saved = block_forward(time_in, w_qkv_time, w_out_time, True)
    returned = lax.all_to_all(time_out[:, None], "seq", split_axis=0, concat_axis=1, tiled=True)
    grad_arrived = lax.all_to_all(grad_parts, "seq", split_axis=1, concat_axis=0, tiled=True)
    d_time_in, g_qkv_time, g_out_time = block_backward(
        time_in, time_saved, grad_arrived[:, 0], w_qkv_time, w_out_time, True
    )
    d_space = lax.all_to_all(d_time_in[:, None], "seq", split_axis=0, concat_axis=1, tiled=True)
    d_space = d_space.reshape(frames_dev, patch_total, feature_count)
    d_video, g_qkv_space, g_out_space = block_backward(
        frames_here, space_saved, d_space, w_qkv_space, w_out_space, False
    )
    reduced = (
        lax.psum_scatter(
            g_qkv_space.astype(jnp.bfloat16), "seq", scatter_dimension=0, tiled=True
        ).astype(jnp.float32),
        lax.psum_scatter(
            g_out_space.astype(jnp.bfloat16), "seq", scatter_dimension=0, tiled=True
        ).astype(jnp.float32),
        lax.psum_scatter(
            g_qkv_time.astype(jnp.bfloat16), "seq", scatter_dimension=0, tiled=True
        ).astype(jnp.float32),
        lax.psum_scatter(
            g_out_time.astype(jnp.bfloat16), "seq", scatter_dimension=0, tiled=True
        ).astype(jnp.float32),
    )
    reduced = (
        lax.psum(reduced[0].astype(jnp.bfloat16), "dp").astype(jnp.float32),
        lax.psum(reduced[1].astype(jnp.bfloat16), "dp").astype(jnp.float32),
        lax.psum(reduced[2].astype(jnp.bfloat16), "dp").astype(jnp.float32),
        lax.psum(reduced[3].astype(jnp.bfloat16), "dp").astype(jnp.float32),
    )
    output_frames = returned.reshape(frames_dev, patch_total, feature_count)[None]
    return (output_frames, d_video[None], reduced[0], reduced[1], reduced[2], reduced[3])


def solution(mesh):
    return jax.shard_map(
        shards,
        mesh=mesh,
        in_specs=(P("dp", "seq", None, None), P(), P(), P(), P(), P("dp", "seq", None, None)),
        out_specs=(
            P("dp", "seq", None, None),
            P("dp", "seq", None, None),
            P("seq", None),
            P("seq", None),
            P("seq", None),
            P("seq", None),
        ),
        check_vma=False,
    )
```

profile of v0, /device:TPU:8, one launch (start us, length us, event | category | flops | bytes accessed | tf_op | source)
XLA Modules:
  0.0 888.7 jit_solution(2593194527215250634)
XLA Ops:
  7.2 9.1 %all-to-all-start.2 = ((bf16[1,32,8,768]{3,2,0,1:T(8,128)(2,1)}), bf16[1,32,8,768]{3,2,0,1:T(8,128)(2,1)}, u32[]{:S(2)}, u32[]{:S(2)}) async-start(bf16[1,32,8,768]{3,2,0,1:T(8,128)(2,1)} %bitcast.216), calls=%async_computation.2 | async-start | bytes 786432 | tf_op jit(solution)/shard_map/all_to_all | solution.py:134
  19.3 4.3 convolution_convert_fusion.3
  23.6 2.4 copy.43
  27.7 2.4 fusion.95
  36.5 7.8 all-to-all-start
  44.5 2.6 convolution_convert_fusion.13
  47.2 2.4 reshape.251
  49.6 8.2 all-to-all-done
  62.7 3.2 convolution_convert_fusion.2
  65.9 4.7 reshape.249
  70.6 4.2 fusion.94
  74.8 4.7 fusion.96
  79.6 5.2 multiply_reduce_fusion.2
  86.9 2.5 reshape.250
  89.4 2.7 convolution_convert_fusion.4
  92.5 3.1 fusion.15
  98.6 2.6 copy.55
  101.2 4.8 reshape.252
  106.0 2.6 fusion.93
  110.1 18.0 %all_to_all.16 = bf16[32,1,8,768]{3,2,1,0:T(8,128)(2,1)S(1)} all-to-all(bf16[32,1,8,768]{3,2,1,0:T(8,128)(2,1)S(1)} %fusion.64), channel_id=1, replica_groups=mesh['dp'=8,'seq'=32] {'seq'}, dimensions={0} | all-to-all | bytes 786432 | tf_op jit(solution)/shard_map/all_to_all | solution.py:138
  129.7 4.0 convolution_convert_fusion
  137.1 2.8 multiply_reduce_fusion
  142.7 3.1 convolution_convert_fusion.1
  149.4 4.6 all-to-all-start.1
  154.0 4.1 fusion.92
  158.1 79.4 %reduce-scatter.11.cloned.1.call-done = bf16[24,768]{1,0:T(8,128)(2,1)} async-done(((bf16[768,768]{1,0:T(8,128)(2,1)}), bf16[24,768]{1,0:T(8,128)(2,1)}) %reduce-scatter.11.cloned.1.call-update) | async-done | bytes 36880 | tf_op jit(solution)/shard_map/reduce_scatter | solution.py:153
  237.5 145.2 %reduce-scatter.7.cloned.1.call-done = bf16[24,768]{1,0:T(8,128)(2,1)} async-done(((bf16[768,768]{1,0:T(8,128)(2,1)}), bf16[24,768]{1,0:T(8,128)(2,1)}) %reduce-scatter.7.cloned.1.call-update) | async-done | bytes 36880 | tf_op jit(solution)/shard_map/reduce_scatter | solution.py:147
  382.8 147.9 %reduce-scatter.9.cloned.1.call-done = bf16[24,2304]{1,0:T(8,128)(2,1)} async-done(((bf16[768,2304]{1,0:T(8,128)(2,1)}), bf16[24,2304]{1,0:T(8,128)(2,1)}) %reduce-scatter.9.cloned.1.call-update) | async-done | bytes 110608 | tf_op jit(solution)/shard_map/reduce_scatter | solution.py:150
  530.7 148.0 %reduce-scatter.5.cloned.1.call-done = bf16[24,2304]{1,0:T(8,128)(2,1)} async-done(((bf16[768,2304]{1,0:T(8,128)(2,1)}), bf16[24,2304]{1,0:T(8,128)(2,1)}) %reduce-scatter.5.cloned.1.call-update) | async-done | bytes 110608 | tf_op jit(solution)/shard_map/reduce_scatter | solution.py:144
  678.7 2.6 fusion.66
  681.2 92.7 %all-reduce.5.cloned.1.call-done = (bf16[24,768]{1,0:T(8,128)(2,1)}, bf16[24,768]{1,0:T(8,128)(2,1)}) async-done(((bf16[24,768]{1,0:T(8,128)(2,1)}, bf16[24,768]{1,0:T(8,128)(2,1)}), (bf16[24,768]{1,0:T(8,128)(2,1)}, bf16[24,768]{1,0:T(8,128)(2,1)})) %all-reduce.5.cloned.1.call-update) | async-done | bytes 73744 | tf_op jit(solution)/shard_map/psum | solution.py:159
  776.7 100.1 %all-reduce.7.cloned.1.call-done = (bf16[24,2304]{1,0:T(8,128)(2,1)}, bf16[24,2304]{1,0:T(8,128)(2,1)}) async-done(((bf16[24,2304]{1,0:T(8,128)(2,1)}, bf16[24,2304]{1,0:T(8,128)(2,1)}), (bf16[24,2304]{1,0:T(8,128)(2,1)}, bf16[24,2304]{1,0:T(8,128)(2,1)})) %all-reduce.7.cloned.1.call-update) | async-done | bytes 221200 | tf_op jit(solution)/shard_map/psum | solution.py:158
  (122 shorter events, 42.2 us)
Async XLA Ops:
  7.2 55.6 %copy-start = (bf16[768,2304]{1,0:T(8,128)(2,1)S(1)}, bf16[768,2304]{1,0:T(8,128)(2,1)}, u32[]{:S(2)}) copy-start(bf16[768,2304]{1,0:T(8,128)(2,1)} %param.9) | copy-start | bytes 10616836
  7.2 29.3 %all-to-all-start.2 = ((bf16[1,32,8,768]{3,2,0,1:T(8,128)(2,1)}), bf16[1,32,8,768]{3,2,0,1:T(8,128)(2,1)}, u32[]{:S(2)}, u32[]{:S(2)}) async-start(bf16[1,32,8,768]{3,2,0,1:T(8,128)(2,1)} %bitcast.216), calls=%async_computation.2 | async-start | bytes 786432 | tf_op jit(solution)/shard_map/all_to_all | solution.py:134
  30.1 1.7 copy-start.6
  30.1 1.7 copy-start.24
  32.9 2.3 copy-start.4
  33.0 2.3 copy-start.9
  36.5 21.3 %all-to-all-start = ((bf16[1,32,8,768]{3,2,0,1:T(8,128)(2,1)}), bf16[1,32,8,768]{3,2,0,1:T(8,128)(2,1)}, u32[]{:S(2)}, u32[]{:S(2)}) async-start(bf16[1,32,8,768]{3,2,0,1:T(8,128)(2,1)} %fusion.30), calls=%async_computation | async-start | bytes 786432 | tf_op jit(solution)/shard_map/all_to_all | solution.py:130
  44.3 193.2 %reduce-scatter.11.cloned.1.call-start = ((), (), s32[]{:S(2)}) async-start(), calls=%async_computation.11 | async-start | bytes 1216512 | tf_op jit(solution)/shard_map/reduce_scatter | solution.py:153
  79.5 5.2 copy-start.18
  92.1 290.6 %reduce-scatter.7.cloned.1.call-start = ((), (), s32[]{:S(2)}) async-start(), calls=%async_computation.9 | async-start | bytes 1216512 | tf_op jit(solution)/shard_map/reduce_scatter | solution.py:147
  92.4 3.1 copy-start.22
  92.4 3.1 copy-start.32
  92.4 3.5 copy-start.33
  92.4 3.5 copy-start.34
  92.4 3.5 copy-start.35
  95.9 1.4 copy-start.20
  106.0 2.7 copy-start.30
  106.0 2.7 copy-start.31
  108.6 19.5 %copy-start.15 = (bf16[12,64,256]{2,1,0:T(8,128)(2,1)S(1)}, bf16[12,64,256]{2,1,0:T(8,128)(2,1)}, u32[]{:S(2)}) copy-start(bf16[12,64,256]{2,1,0:T(8,128)(2,1)} %copy-done.14) | copy-start | bytes 1179652
  128.1 6.0 copy-start.8
  128.1 1.6 copy-start.13
  128.1 1.6 copy-start.23
  129.7 401.0 %reduce-scatter.9.cloned.1.call-start = ((), (), s32[]{:S(2)}) async-start(), calls=%async_computation.10 | async-start | bytes 3649536 | tf_op jit(solution)/shard_map/reduce_scatter | solution.py:150
  133.8 2.7 copy-start.3
  133.8 544.9 %reduce-scatter.5.cloned.1.call-start = ((), (), s32[]{:S(2)}) async-start(), calls=%async_computation.8 | async-start | bytes 3649536 | tf_op jit(solution)/shard_map/reduce_scatter | solution.py:144
  135.5 1.5 copy-start.25
  135.7 1.4 copy-start.12
  137.1 3.0 copy-start.7
  149.4 233.4 %all-to-all-start.1 = ((bf16[32,1,8,768]{3,2,1,0:T(8,128)(2,1)}), bf16[32,1,8,768]{3,2,1,0:T(8,128)(2,1)}, u32[]{:S(2)}, u32[]{:S(2)}) async-start(bf16[32,1,8,768]{3,2,1,0:T(8,128)(2,1)} %fusion.29), calls=%async_computation.1 | async-start | bytes 786432 | tf_op jit(solution)/shard_map/all_to_all | solution.py:133
  154.0 620.0 %all-reduce.5.cloned.1.call-start = ((), (), s32[]{:S(2)}) async-start(), calls=%async_computation.12 | async-start | bytes 147456 | tf_op jit(solution)/shard_map/psum | solution.py:159
  382.8 494.1 %all-reduce.7.cloned.1.call-start = ((), (), s32[]{:S(2)}) async-start(), calls=%async_computation.13 | async-start | bytes 442368 | tf_op jit(solution)/shard_map/psum | solution.py:158
  678.7 203.2 %copy-start.1 = (bf16[768,2304]{1,0:T(8,128)(2,1)S(1)}, bf16[768,2304]{1,0:T(8,128)(2,1)}, u32[]{:S(2)}) copy-start(bf16[768,2304]{1,0:T(8,128)(2,1)} %param.9) | copy-start | bytes 10616836
  (13 other events, 13.4 us)
Sparse Core Ops, SparseCore 0:
  92.3 145.2 reduce-scatter.10
  240.2 142.5 reduce-scatter.6
  385.3 145.3 reduce-scatter.8
  533.2 145.3 reduce-scatter.4
  681.2 92.7 all-reduce.4
  776.7 100.1 all-reduce.6
where the time goes:
time: 893 us; the launch traced here: 889 us
  waiting for transfers between devices  722 us (81%)
  matrix products  55.5 us (6%)
  local copies, waits for them, and re-layouts  37.9 us (4%)
  starting transfers between devices  22.4 us (3%)
  other arithmetic  18.8 us (2%)
  blocking collectives  18 us (2%)
  between operations  14.6 us (2%)
    reduce_scatter x1, waiting for transfers between devices, shards(): lax.psum_scatter(g_qkv_space.astype(jnp.bfloat16), 'seq', scatter_dimensi...  148 us
    reduce_scatter x1, waiting for transfers between devices, shards(): lax.psum_scatter(g_qkv_time.astype(jnp.bfloat16), 'seq', scatter_dimensio...  148 us
    reduce_scatter x1, waiting for transfers between devices, shards(): lax.psum_scatter(g_out_space.astype(jnp.bfloat16), 'seq', scatter_dimensi...  145 us
    psum x1, waiting for transfers between devices, shards(): lax.psum(reduced[0].astype(jnp.bfloat16), 'dp').astype(jnp.float32)  100 us
    psum x1, waiting for transfers between devices, shards(): lax.psum(reduced[1].astype(jnp.bfloat16), 'dp').astype(jnp.float32)  92.7 us
    reduce_scatter x1, waiting for transfers between devices, shards(): lax.psum_scatter(g_out_time.astype(jnp.bfloat16), 'seq', scatter_dimensio...  79.4 us
    all_to_all x1, blocking collectives, shards(): lax.all_to_all(d_time_in[:, None], 'seq', split_axis=0, concat_axis=1, ti...  18 us
  transfers between devices with their start and end apart: 9, of which 7 were waited for; matrix products, arithmetic and copies ran while one was open for 7% of the time, Pallas kernels for 0%

commit v1 on v0

v1 whole, which is shorter than its diff:
```python
import math

import jax
import jax.numpy as jnp
from jax import lax
from jax.experimental import pallas as pl
from jax.experimental.pallas import tpu as pltpu
from jax.sharding import PartitionSpec as P

MESH = pl.DeviceIdType.MESH
F32 = jnp.float32
BF16 = jnp.bfloat16
HD = 64
D = 768
ROWS = 256
PAIRS = 6
GROUP = 32
EPSILON = 1e-05
SCALE = 1.0 / math.sqrt(HD)
SCALE_LOG2E = SCALE * math.log2(math.e)
ORDERS = ("xyz", "yzx", "zxy")
TIME, SPACE = 0, 1


def place(x, y, z, c):
    return ((z // 4) * 4 + y, (z % 4) * 8 + x * 2 + c)


def mm(a, b):
    return jnp.dot(a, b, preferred_element_type=F32)


def mm_nt(a, b):
    return lax.dot_general(a, b, (((1,), (1,)), ((), ())), preferred_element_type=F32)


def mm_tn(a, b):
    return lax.dot_general(a, b, (((0,), (0,)), ((), ())), preferred_element_type=F32)


def normalize(rows):
    mean = jnp.mean(rows, axis=-1, keepdims=True)
    centred = rows - mean
    variance = jnp.mean(centred * centred, axis=-1, keepdims=True)
    inverse = lax.rsqrt(variance + EPSILON)
    return centred * inverse, inverse


def normalize_back(rows, d_normed):
    normed, inverse = normalize(rows)
    d_centre = jnp.mean(d_normed, axis=-1, keepdims=True)
    d_spread = jnp.mean(d_normed * normed, axis=-1, keepdims=True)
    return inverse * (d_normed - d_centre - normed * d_spread)


def pack(rows):
    cut = rows.reshape(GROUP, 8, D)
    return jnp.concatenate([cut[:, :, : D // 2], cut[:, :, D // 2 :]], axis=1).astype(BF16)


def unpack(blocks):
    wide = blocks.astype(F32)
    return jnp.concatenate([wide[:, :8], wide[:, 8:]], axis=2).reshape(ROWS, D)


def softmax(scores):
    highest = jnp.max(scores, axis=-1, keepdims=True)
    weights = jnp.exp2((scores - highest) * SCALE_LOG2E)
    return weights * (1.0 / jnp.sum(weights, axis=-1, keepdims=True))


def kernel(
    video, wqs, wos, wqt, wot, gout,
    out_video, grad_video, oqs, oos, oqt, oot,
    vid_v, gout_v, wqs_v, wos_v, wqt_v, wot_v,
    qkv_s, qkv_t, att_s, att_t, dqkv, datt, tin, gt, nT, aT, nTs, aTs,
    probs_s, probs_t, perm, permT, outv, gradv,
    sbuf, rbuf, G, r1, r2, b, r3, cc, r4, d, r5, e, f,
    lsem, asem, arsem, ssem, rsem,
):
    dp, seq = lax.axis_index("dp"), lax.axis_index("seq")
    x, y, z, c = (seq // 2) % 4, dp % 4, (dp // 4) * 4 + seq // 8, seq % 2
    tie = 1 - 2 * (z % 2)
    xs = [place((x + k) % 4, y, z, c) for k in (1, 2, 3)]
    ys = [place(x, (y + k) % 4, z, c) for k in (1, 2, 3)]
    zoff = [1, 7, (8 + 2 * tie) % 8]
    zt = [place(x, y, (z + o) % 8, c) for o in zoff]
    zs = [place(x, y, (z + 8 - o) % 8, c) for o in zoff]
    zh = place(x, y, (z + 4) % 8, c)
    core = place(x, y, z, 1 - c)
    targets = {
        "x": [(p, (x + k) % 4) for p, k in zip(xs, (1, 2, 3))],
        "y": [(p, (y + k) % 4) for p, k in zip(ys, (1, 2, 3))],
        "z": [(p, (z + o) % 4) for p, o in zip(zt, zoff)],
    }
    own = {"x": x, "y": y, "z": z % 4}

    loads = [
        pltpu.make_async_copy(src, dst, lsem.at[i])
        for i, (src, dst) in enumerate(
            ((video, vid_v), (wqs, wqs_v), (wos, wos_v), (gout, gout_v), (wqt, wqt_v), (wot, wot_v))
        )
    ]
    for load in loads:
        load.start()

    barrier = pltpu.get_barrier_semaphore()

    def greet(k, _):
        pl.semaphore_signal(barrier, inc=1, device_id=(dp, (seq + k) % GROUP), device_id_type=MESH)
        return 0

    lax.fori_loop(1, GROUP, greet, 0)
    for peer in ys + zs + [zh]:
        pl.semaphore_signal(barrier, inc=1, device_id=peer, device_id_type=MESH)

    def done(ref, sem):
        pltpu.make_async_copy(ref, ref, sem).wait()

    def exchange(i):
        def one(k, _):
            to = (seq + k) % GROUP
            pltpu.make_async_remote_copy(
                sbuf.at[i, to], rbuf.at[i, seq], asem.at[i], arsem.at[i],
                device_id=(dp, to), device_id_type=MESH,
            ).start()
            return 0

        lax.fori_loop(1, GROUP, one, 0)
        rbuf[i, seq] = sbuf[i, seq]

    def arrived(i):
        done(rbuf.at[i, pl.ds(0, GROUP - 1)], arsem.at[i])

    def send(src, dst, h, s, dev):
        pltpu.make_async_remote_copy(
            src, dst, ssem.at[h, s], rsem.at[h, s], device_id=dev, device_id_type=MESH
        ).start()

    def sum_core_start(h):
        send(G.at[h, 1 - c], r1.at[h], h, 0, core)

    def sum_first(h):
        done(r1.at[h], rsem.at[h, 0])
        for j in range(3):
            def body(i, _):
                r1[h, j, i] = (G[h, c, j, i].astype(F32) + r1[h, j, i].astype(F32)).astype(BF16)
                return 0

            lax.fori_loop(0, 4, body, 0)
            for k, (dev, o) in enumerate(targets[ORDERS[j][0]]):
                send(r1.at[h, j, o], r2.at[h, j, k], h, 1 + j, dev)

    def sum_second(h):
        for j in range(3):
            done(r2.at[h, j], rsem.at[h, 1 + j])
            o0 = own[ORDERS[j][0]]

            def body(i, _):
                t = r1[h, j, o0, i].astype(F32)
                for k in range(3):
                    t = t + r2[h, j, k, i].astype(F32)
                b[h, j, i] = t.astype(BF16)
                return 0

            lax.fori_loop(0, 4, body, 0)
            for k, (dev, o) in enumerate(targets[ORDERS[j][1]]):
                send(b.at[h, j, o], r3.at[h, j, k], h, 4 + j, dev)

    def sum_third(h):
        for j in range(3):
            done(r3.at[h, j], rsem.at[h, 4 + j])
            t = b[h, j, own[ORDERS[j][1]]].astype(F32)
            for k in range(3):
                t = t + r3[h, j, k].astype(F32)
            cc[h, j] = t.astype(BF16)
            for k, (dev, o) in enumerate(targets[ORDERS[j][2]]):
                send(cc.at[h, j, o], r4.at[h, j, k], h, 7 + j, dev)

    def sum_far(h):
        for j in range(3):
            done(r4.at[h, j], rsem.at[h, 7 + j])
            t = cc[h, j, own[ORDERS[j][2]]].astype(F32)
            for k in range(3):
                t = t + r4[h, j, k].astype(F32)
            d[h, j] = t.astype(BF16)
        send(d.at[h], r5.at[h], h, 10, zh)

    def sum_gather(h):
        done(r5.at[h], rsem.at[h, 10])
        e[h] = (d[h].astype(F32) + r5[h].astype(F32)).astype(BF16)
        for k, dev in enumerate(ys):
            send(e.at[h], f.at[h, k], h, 11, dev)

    def sum_finish(h, wide_out, narrow_out):
        done(f.at[h], rsem.at[h, 11])
        for k in range(4):
            block = (e[h] if k == 0 else f[h, k - 1]).astype(F32).reshape(48, D // 2)
            source = (y + 4 - k) % 4
            for t in range(4):
                @pl.when(source == t)
                def _():
                    out, at = (wide_out, D * t) if t < 3 else (narrow_out, 0)
                    out[:, at : at + D // 2] = block[:24]
                    out[:, at + D // 2 : at + D] = block[24:]

    def sum_sent(h):
        done(r1.at[h], ssem.at[h, 0])
        for j in range(3):
            done(r2.at[h, j], ssem.at[h, 1 + j])
            done(r3.at[h, j], ssem.at[h, 4 + j])
            done(r4.at[h, j], ssem.at[h, 7 + j])
        done(r5.at[h], ssem.at[h, 10])
        done(f.at[h], ssem.at[h, 11])

    def write_grad(h, left, right, part):
        def body(zp, _):
            block = mm(left[pl.ds(pl.multiple_of(192 * zp, 16), 192), :], right)
            for i in range(8):
                xp, cp = i // 2, i % 2
                own_rows = block[24 * i : 24 * i + 24]
                own_rows = jnp.concatenate([own_rows[:, : D // 2], own_rows[:, D // 2 :]], axis=0).astype(BF16)
                G[h, cp, 0, xp, part, zp] = own_rows[0:16]
                G[h, cp, 1, part, zp, xp] = own_rows[16:32]
                G[h, cp, 2, zp, xp, part] = own_rows[32:48]
            return 0

        lax.fori_loop(0, 4, body, 0)

    left_half = lax.broadcasted_iota(jnp.int32, (1, 128), 1) < HD

    def halves(value):
        zero = jnp.zeros_like(value)
        return jnp.where(left_half, value, zero), jnp.where(left_half, zero, value)

    def columns(pair, part):
        return pl.ds(pl.multiple_of(part * D + pair * 128, 128), 128)

    def attend(qkv, probs, att, size, mask):
        def body(pair, _):
            for blk in range(ROWS // size):
                rows = slice(blk * size, blk * size + size)
                queries = halves(qkv[rows, columns(pair, 0)])
                keys = qkv[rows, columns(pair, 1)]
                values = halves(qkv[rows, columns(pair, 2)])
                total = None
                for s in range(2):
                    scores = mm_nt(queries[s], keys)
                    if mask is not None:
                        scores = jnp.where(mask, scores, -1e30)
                    low = softmax(scores).astype(BF16)
                    probs[pair * 2 + s, rows] = low
                    part = mm(low, values[s])
                    total = part if total is None else total + part
                att[rows, columns(pair, 0)] = total.astype(BF16)
            return 0

        lax.fori_loop(0, PAIRS, body, 0)

    def attend_back(qkv, probs, size, first, last):
        def body(pair, _):
            for blk in range(ROWS // size):
                rows = slice(blk * size, blk * size + size)
                queries = halves(qkv[rows, columns(pair, 0)])
                keys = halves(qkv[rows, columns(pair, 1)])
                values = qkv[rows, columns(pair, 2)]
                d_out = halves(datt[rows, columns(pair, 0)])
                d_queries = d_keys = d_values = 0.0
                for s in range(2):
                    low = probs[pair * 2 + s, rows]
                    wide = low.astype(F32)
                    d_probs = mm_nt(d_out[s], values)
                    product = d_probs * wide
                    d_scores = (product - wide * jnp.sum(product, axis=-1, keepdims=True)).astype(BF16)
                    d_values = d_values + mm_tn(low, d_out[s])
                    d_queries = d_queries + mm(d_scores, keys[s])
                    d_keys = d_keys + mm_tn(d_scores, queries[s])
                dqkv[rows, columns(pair, 0)] = (d_queries * SCALE).astype(BF16)
                dqkv[rows, columns(pair, 1)] = (d_keys * SCALE).astype(BF16)
                dqkv[rows, columns(pair, 2)] = d_values.astype(BF16)
            return 0

        lax.fori_loop(first, last, body, 0)

    def project(normed, weights, qkv):
        for part in range(3):
            at = slice(part * D, part * D + D)
            qkv[:, at] = mm(normed, weights[:, at]).astype(BF16)

    def project_back(weights):
        total = mm_nt(dqkv[:, :D], weights[:, :D])
        for part in (1, 2):
            at = slice(part * D, part * D + D)
            total = total + mm_nt(dqkv[:, at], weights[:, at])
        return total

    loads[0].wait()
    rows_in = vid_v[...].astype(F32)
    normed = normalize(rows_in)[0].astype(BF16)
    loads[1].wait()
    project(normed, wqs_v, qkv_s)
    nTs[...] = normed.T
    loads[3].wait()
    sbuf[0] = pack(gout_v[...].astype(F32))
    pl.semaphore_wait(barrier, GROUP - 1 + 7)
    exchange(0)
    attend(qkv_s, probs_s, att_s, ROWS, None)
    loads[2].wait()
    sbuf[1] = pack(vid_v[...].astype(F32) + mm(att_s[...], wos_v[...]))
    exchange(1)

    r = lax.broadcasted_iota(jnp.int32, (ROWS, ROWS), 0)
    q = lax.broadcasted_iota(jnp.int32, (ROWS, ROWS), 1)
    perm[...] = jnp.where(q == (r % 32) * 8 + r // 32, 1.0, 0.0).astype(BF16)
    permT[...] = jnp.where(r == (q % 32) * 8 + q // 32, 1.0, 0.0).astype(BF16)
    aTs[...] = att_s[...].T
    arrived(0)
    gt[...] = mm(perm[...], unpack(rbuf[0]).astype(BF16)).astype(BF16)
    loads[4].wait()
    loads[5].wait()
    datt[...] = mm_nt(gt[...], wot_v[...]).astype(BF16)
    arrived(1)

    rows_in = mm(perm[...], unpack(rbuf[1]).astype(BF16))
    tin[...] = rows_in.astype(BF16)
    normed = normalize(rows_in)[0].astype(BF16)
    project(normed, wqt_v, qkv_t)
    nT[...] = normed.T
    same = (
        lax.broadcasted_iota(jnp.int32, (128, 128), 0) // 32
        == lax.broadcasted_iota(jnp.int32, (128, 128), 1) // 32
    )
    attend(qkv_t, probs_t, att_t, 128, same)
    low = (tin[...].astype(F32) + mm(att_t[...], wot_v[...])).astype(BF16)
    sbuf[2] = pack(mm(permT[...], low))
    exchange(2)
    attend_back(qkv_t, probs_t, 128, 0, PAIRS)
    d_rows = normalize_back(tin[...].astype(F32), project_back(wqt_v))
    low = (gt[...].astype(F32) + d_rows).astype(BF16)
    sbuf[3] = pack(mm(permT[...], low))
    exchange(3)
    aT[...] = att_t[...].T
    for part in range(3):
        write_grad(TIME, nT, dqkv[:, part * D : part * D + D], part)
    write_grad(TIME, aT, gt[...], 3)
    sum_core_start(TIME)
    arrived(2)
    outv[...] = unpack(rbuf[2]).astype(BF16)
    out_copy = pltpu.make_async_copy(outv, out_video, lsem.at[6])
    out_copy.start()
    arrived(3)

    d_space = unpack(rbuf[3]).astype(BF16)
    datt[...] = mm_nt(d_space, wos_v[...]).astype(BF16)
    write_grad(SPACE, aTs, d_space, 3)
    attend_back(qkv_s, probs_s, ROWS, 0, 2)
    sum_first(TIME)
    attend_back(qkv_s, probs_s, ROWS, 2, 4)
    sum_second(TIME)
    attend_back(qkv_s, probs_s, ROWS, 4, 6)
    sum_third(TIME)
    for part in range(3):
        write_grad(SPACE, nTs, dqkv[:, part * D : part * D + D], part)
    sum_core_start(SPACE)
    sum_far(TIME)
    d_rows = normalize_back(vid_v[...].astype(F32), project_back(wqs_v))
    gradv[...] = (unpack(rbuf[3]) + d_rows).astype(BF16)
    grad_copy = pltpu.make_async_copy(gradv, grad_video, lsem.at[7])
    grad_copy.start()
    sum_gather(TIME)
    sum_first(SPACE)
    sum_finish(TIME, oqt, oot)
    sum_second(SPACE)
    sum_third(SPACE)
    sum_far(SPACE)
    sum_gather(SPACE)
    sum_finish(SPACE, oqs, oos)
    for i in range(4):
        done(rbuf.at[i, pl.ds(0, GROUP - 1)], asem.at[i])
    sum_sent(TIME)
    sum_sent(SPACE)
    out_copy.wait()
    grad_copy.wait()


def shards(video, w_qkv_space, w_out_space, w_qkv_time, w_out_time, grad_out):
    V = lambda *s: pltpu.VMEM(s, BF16)
    anywhere = pl.BlockSpec(memory_space=pl.ANY)
    vmem = pl.BlockSpec(memory_space=pltpu.VMEM)
    tokens = jax.ShapeDtypeStruct((ROWS, D), BF16)
    wide = jax.ShapeDtypeStruct((24, 3 * D), F32)
    narrow = jax.ShapeDtypeStruct((24, D), F32)
    outs = pl.pallas_call(
        kernel,
        out_shape=[tokens, tokens, wide, narrow, wide, narrow],
        in_specs=[anywhere] * 6,
        out_specs=[anywhere] * 2 + [vmem] * 4,
        scratch_shapes=[
            V(ROWS, D), V(ROWS, D), V(D, 3 * D), V(D, D), V(D, 3 * D), V(D, D),
            V(ROWS, 3 * D), V(ROWS, 3 * D), V(ROWS, D), V(ROWS, D), V(ROWS, 3 * D), V(ROWS, D),
            V(ROWS, D), V(ROWS, D), V(D, ROWS), V(D, ROWS), V(D, ROWS), V(D, ROWS),
            V(12, ROWS, ROWS), V(12, ROWS, 128), V(ROWS, ROWS), V(ROWS, ROWS), V(ROWS, D), V(ROWS, D),
            V(4, GROUP, 16, 384), V(4, GROUP, 16, 384),
            V(2, 2, 3, 4, 4, 4, 16, 384), V(2, 3, 4, 4, 4, 16, 384), V(2, 3, 3, 4, 4, 16, 384),
            V(2, 3, 4, 4, 16, 384), V(2, 3, 3, 4, 16, 384), V(2, 3, 4, 16, 384), V(2, 3, 3, 16, 384),
            V(2, 3, 16, 384), V(2, 3, 16, 384), V(2, 3, 16, 384), V(2, 3, 3, 16, 384),
            pltpu.SemaphoreType.DMA((8,)), pltpu.SemaphoreType.DMA((4,)), pltpu.SemaphoreType.DMA((4,)),
            pltpu.SemaphoreType.DMA((2, 12)), pltpu.SemaphoreType.DMA((2, 12)),
        ],
        compiler_params=pltpu.CompilerParams(
            collective_id=0, has_side_effects=True, vmem_limit_bytes=60 * 2**20
        ),
        name="layer",
    )(
        video.reshape(ROWS, D), w_qkv_space, w_out_space, w_qkv_time, w_out_time, grad_out.reshape(ROWS, D)
    )
    shape = (1, 1, ROWS, D)
    return (outs[0].reshape(shape), outs[1].reshape(shape), outs[2], outs[3], outs[4], outs[5])


def solution(mesh):
    return jax.shard_map(
        shards,
        mesh=mesh,
        in_specs=(P("dp", "seq", None, None), P(), P(), P(), P(), P("dp", "seq", None, None)),
        out_specs=(
            P("dp", "seq", None, None),
            P("dp", "seq", None, None),
            P("seq", None),
            P("seq", None),
            P("seq", None),
            P("seq", None),
        ),
        check_vma=False,
    )
```

time: 893 us -> 126 us (0.14)
  waiting for transfers between devices: 722 us -> 0 us
  Pallas kernels: 0 us -> 115 us
  matrix products: 55.5 us -> 0 us
  local copies, waits for them, and re-layouts: 37.9 us -> 9.84 us
  starting transfers between devices: 22.4 us -> 0 us
  other arithmetic: 18.8 us -> 0 us
  blocking collectives: 18 us -> 0 us
  between operations: 14.6 us -> 0.64 us
    reduce_scatter x4 -> x0, waiting for transfers between devices: 520 us -> none  [the longest x1 148 us: shards(): lax.psum_scatter(g_qkv_space.astype(jnp.bfloat16), 'seq', scatter_dimensi...]
    psum x2 -> x0, waiting for transfers between devices: 193 us -> none  [the longest x1 100 us: shards(): lax.psum(reduced[0].astype(jnp.bfloat16), 'dp').astype(jnp.float32)]
    pallas_call x0 -> x1, Pallas kernels: none -> 115 us  [shards(): pl.pallas_call(kernel, out_shape=[tokens, tokens, wide, narrow, wide, nar...]
    dot_general x23 -> x0, matrix products: 50.7 us -> none  [the longest x2 8.04 us: attend_back(): jnp.einsum(query_form + ',' + key_form + '->bhlm', d_wide, values.astype(...]
    all_to_all x3 -> x0, starting transfers between devices: 21.5 us -> none  [the longest x1 9.14 us: shards(): lax.all_to_all(grad_parts, 'seq', split_axis=1, concat_axis=0, tiled=True)]
    all_to_all x1 -> x0, blocking collectives: 18 us -> none  [shards(): lax.all_to_all(d_time_in[:, None], 'seq', split_axis=0, concat_axis=1, ti...]
    reshape x4 -> x0, local copies, waits for them, and re-layouts: 14.4 us -> none  [the longest x1 4.76 us: block_backward(): jnp.stack([d_queries, d_keys, d_values], axis=2)]
  transfers between devices with their start and end apart: 9 -> 0, of which waited for: 7 -> 0; matrix products, arithmetic and copies ran while one was open for 7% -> 0% of each run, Pallas kernels for 0% -> 0%
where the time goes in v1:
time: 126 us; the launch traced here: 125 us
  Pallas kernels  115 us (91%)
  local copies, waits for them, and re-layouts  9.84 us (8%)
    pallas_call x1, Pallas kernels, shards(): pl.pallas_call(kernel, out_shape=[tokens, tokens, wide, narrow, wide, nar...  115 us
    unnamed x6, local copies, waits for them, and re-layouts  9.84 us

profile of v1, /device:TPU:8, one launch (start us, length us, event | category | flops | bytes accessed | tf_op | source)
XLA Modules:
  0.0 125.2 jit_solution(9881280978433856621)
XLA Ops:
  0.6 114.7 %layer.1 = (bf16[256,768]{1,0:T(8,128)(2,1)}, bf16[256,768]{1,0:T(8,128)(2,1)}, f32[24,2304]{1,0:T(8,128)}, f32[24,768]{1,0:T(8,128)}, f32[24,2304]{1,0:T(8,128)}, /*index=5*/f32[24,768]{1,0:T(8,128)}) custom-call(bf16[256,768]{1,0:T(8,128)(2,1)} %bitcast.4, bf16[768,2304]{1,0:T(8,128)(2,1)} %wqs.1, bf16[768,768]{1,0:T(8,128)(2,1)} %wos.1, ...), custom_call_target="tpu_custom_call" | custom-call | tf_op jit(solution)/shard_map/layer/pallas_call | solution.py:393
  115.4 1.8 %copy.18 = bf16[1,1,256,768]{3,2,1,0:T(8,128)(2,1)} copy(bf16[1,1,256,768]{3,2,1,0:T(8,128)(2,1)} %bitcast.7) | data formatting | bytes 786432
  117.2 1.8 %copy.19 = bf16[1,1,256,768]{3,2,1,0:T(8,128)(2,1)} copy(bf16[1,1,256,768]{3,2,1,0:T(8,128)(2,1)} %bitcast.6) | data formatting | bytes 786432
  118.9 1.6 %copy.20 = f32[24,2304]{1,0:T(8,128)} copy(f32[24,2304]{1,0:T(8,128)} %get-tuple-element.26) | data formatting | bytes 442368
  120.6 1.5 %copy.21 = f32[24,768]{1,0:T(8,128)} copy(f32[24,768]{1,0:T(8,128)} %get-tuple-element.27) | data formatting | bytes 147456
  122.1 1.6 %copy.22 = f32[24,2304]{1,0:T(8,128)} copy(f32[24,2304]{1,0:T(8,128)} %get-tuple-element.28) | data formatting | bytes 442368
  123.7 1.5 %copy.23 = f32[24,768]{1,0:T(8,128)} copy(f32[24,768]{1,0:T(8,128)} %get-tuple-element.29) | data formatting | bytes 147456

commit v2 on v1

--- a/solution.py
+++ b/solution.py
@@ -1,3 +1,4 @@
+import itertools
 import math
 
 import jax
@@ -12,14 +13,18 @@
 BF16 = jnp.bfloat16
 HD = 64
 D = 768
+HALF = 384
 ROWS = 256
 PAIRS = 6
 GROUP = 32
 EPSILON = 1e-05
 SCALE = 1.0 / math.sqrt(HD)
 SCALE_LOG2E = SCALE * math.log2(math.e)
-ORDERS = ("xyz", "yzx", "zxy")
 TIME, SPACE = 0, 1
+ORDERS = (
+    (("xyz", "yzx", "xzy"), ("xyz", "yzx", "yxz")),
+    (("xyz", "yzx", "zxy"), ("xyz", "yzx", "zxy")),
+)
 
 
 def place(x, y, z, c):
@@ -74,7 +79,7 @@
     out_video, grad_video, oqs, oos, oqt, oot,
     vid_v, gout_v, wqs_v, wos_v, wqt_v, wot_v,
     qkv_s, qkv_t, att_s, att_t, dqkv, datt, tin, gt, nT, aT, nTs, aTs,
-    probs_s, probs_t, perm, permT, outv, gradv,
+    probs_s, probs_t, perm, permT, outv, gradv, d_space,
     sbuf, rbuf, G, r1, r2, b, r3, cc, r4, d, r5, e, f,
     lsem, asem, arsem, ssem, rsem,
 ):
@@ -101,8 +106,8 @@
             ((video, vid_v), (wqs, wqs_v), (wos, wos_v), (gout, gout_v), (wqt, wqt_v), (wot, wot_v))
         )
     ]
-    for load in loads:
-        load.start()
+    for i in (0, 3, 1, 2):
+        loads[i].start()
 
     barrier = pltpu.get_barrier_semaphore()
 
@@ -117,115 +122,144 @@
     def done(ref, sem):
         pltpu.make_async_copy(ref, ref, sem).wait()
 
-    def exchange(i):
+    def exchange(i, first=1, last=GROUP):
         def one(k, _):
-            to = (seq + k) % GROUP
+            far = GROUP - k
+            to = ((seq // 8 + far // 8) % 4) * 8 + (x + far // 2) % 4 * 2 + (c + far) % 2
             pltpu.make_async_remote_copy(
                 sbuf.at[i, to], rbuf.at[i, seq], asem.at[i], arsem.at[i],
                 device_id=(dp, to), device_id_type=MESH,
             ).start()
             return 0
 
-        lax.fori_loop(1, GROUP, one, 0)
-        rbuf[i, seq] = sbuf[i, seq]
+        lax.fori_loop(first, last, one, 0)
+        if first == 1:
+            rbuf[i, seq] = sbuf[i, seq]
 
     def arrived(i):
         done(rbuf.at[i, pl.ds(0, GROUP - 1)], arsem.at[i])
 
-    def send(src, dst, h, s, dev):
+    def send(src, dst, h, t, s, dev):
         pltpu.make_async_remote_copy(
-            src, dst, ssem.at[h, s], rsem.at[h, s], device_id=dev, device_id_type=MESH
+            src, dst, ssem.at[h, t, s], rsem.at[h, t, s], device_id=dev, device_id_type=MESH
         ).start()
 
-    def sum_core_start(h):
-        send(G.at[h, 1 - c], r1.at[h], h, 0, core)
-
-    def sum_first(h):
-        done(r1.at[h], rsem.at[h, 0])
+    def sum_core_start(h, t):
+        send(G.at[h, t, 1 - c], r1.at[h, t], h, t, 0, core)
+
+    def sum_add(h, t):
+        done(r1.at[h, t], rsem.at[h, t, 0])
         for j in range(3):
             def body(i, _):
-                r1[h, j, i] = (G[h, c, j, i].astype(F32) + r1[h, j, i].astype(F32)).astype(BF16)
+                r1[h, t, j, i] = (G[h, t, c, j, i].astype(F32) + r1[h, t, j, i].astype(F32)).astype(BF16)
                 return 0
 
-            lax.fori_loop(0, 4, body, 0)
-            for k, (dev, o) in enumerate(targets[ORDERS[j][0]]):
-                send(r1.at[h, j, o], r2.at[h, j, k], h, 1 + j, dev)
-
-    def sum_second(h):
+            lax.fori_loop(0, 4, body, 0, unroll=True)
+
+    def sum_first(h, t, thirds=(0, 1, 2)):
+        for j in thirds:
+            for k, (dev, o) in enumerate(targets[ORDERS[h][t][j][0]]):
+                send(r1.at[h, t, j, o], r2.at[h, t, j, k], h, t, 1 + j, dev)
+
+    def sum_second(h, t):
         for j in range(3):
-            done(r2.at[h, j], rsem.at[h, 1 + j])
-            o0 = own[ORDERS[j][0]]
+            done(r2.at[h, t, j], rsem.at[h, t, 1 + j])
+            o0 = own[ORDERS[h][t][j][0]]
 
             def body(i, _):
-                t = r1[h, j, o0, i].astype(F32)
+                total = r1[h, t, j, o0, i].astype(F32)
                 for k in range(3):
-                    t = t + r2[h, j, k, i].astype(F32)
-                b[h, j, i] = t.astype(BF16)
+                    total = total + r2[h, t, j, k, i].astype(F32)
+                b[h, t, j, i] = total.astype(BF16)
                 return 0
 
-            lax.fori_loop(0, 4, body, 0)
-            for k, (dev, o) in enumerate(targets[ORDERS[j][1]]):
-                send(b.at[h, j, o], r3.at[h, j, k], h, 4 + j, dev)
-
-    def sum_third(h):
+            lax.fori_loop(0, 4, body, 0, unroll=True)
+            for k, (dev, o) in enumerate(targets[ORDERS[h][t][j][1]]):
+                send(b.at[h, t, j, o], r3.at[h, t, j, k], h, t, 4 + j, dev)
+
+    def sum_third(h, t):
         for j in range(3):
-            done(r3.at[h, j], rsem.at[h, 4 + j])
-            t = b[h, j, own[ORDERS[j][1]]].astype(F32)
+            done(r3.at[h, t, j], rsem.at[h, t, 4 + j])
+            total = b[h, t, j, own[ORDERS[h][t][j][1]]].astype(F32)
             for k in range(3):
-                t = t + r3[h, j, k].astype(F32)
-            cc[h, j] = t.astype(BF16)
-            for k, (dev, o) in enumerate(targets[ORDERS[j][2]]):
-                send(cc.at[h, j, o], r4.at[h, j, k], h, 7 + j, dev)
-
-    def sum_far(h):
+                total = total + r3[h, t, j, k].astype(F32)
+            for o in range(4):
+                piece = total[o // 2, 24 * (o % 2) : 24 * (o % 2) + 24]
+                piece = jnp.concatenate([piece, jnp.zeros((8, 128), F32)], axis=0)
+                cc[h, t, j, o] = piece.astype(BF16)
+            for k, (dev, o) in enumerate(targets[ORDERS[h][t][j][2]]):
+                send(cc.at[h, t, j, o], r4.at[h, t, j, k], h, t, 7 + j, dev)
+
+    def sum_far(h, t):
         for j in range(3):
-            done(r4.at[h, j], rsem.at[h, 7 + j])
-            t = cc[h, j, own[ORDERS[j][2]]].astype(F32)
+            done(r4.at[h, t, j], rsem.at[h, t, 7 + j])
+            total = cc[h, t, j, own[ORDERS[h][t][j][2]]].astype(F32)
             for k in range(3):
-                t = t + r4[h, j, k].astype(F32)
-            d[h, j] = t.astype(BF16)
-        send(d.at[h], r5.at[h], h, 10, zh)
-
-    def sum_gather(h):
-        done(r5.at[h], rsem.at[h, 10])
-        e[h] = (d[h].astype(F32) + r5[h].astype(F32)).astype(BF16)
+                total = total + r4[h, t, j, k].astype(F32)
+            d[h, t, j] = total.astype(BF16)
+        send(d.at[h, t], r5.at[h, t], h, t, 10, zh)
+
+    def sum_gather(h, t):
+        done(r5.at[h, t], rsem.at[h, t, 10])
+        e[h, t] = (d[h, t].astype(F32) + r5[h, t].astype(F32)).astype(BF16)
         for k, dev in enumerate(ys):
-            send(e.at[h], f.at[h, k], h, 11, dev)
-
-    def sum_finish(h, wide_out, narrow_out):
-        done(f.at[h], rsem.at[h, 11])
+            send(e.at[h, t], f.at[h, t, k], h, t, 11, dev)
+
+    def sum_finish(h, t, wide_out, narrow_out):
+        done(f.at[h, t], rsem.at[h, t, 11])
         for k in range(4):
-            block = (e[h] if k == 0 else f[h, k - 1]).astype(F32).reshape(48, D // 2)
+            block = (e[h, t] if k == 0 else f[h, t, k - 1]).astype(F32)
             source = (y + 4 - k) % 4
-            for t in range(4):
-                @pl.when(source == t)
+            for part in range(4):
+                @pl.when(source == part)
                 def _():
-                    out, at = (wide_out, D * t) if t < 3 else (narrow_out, 0)
-                    out[:, at : at + D // 2] = block[:24]
-                    out[:, at + D // 2 : at + D] = block[24:]
-
-    def sum_sent(h):
-        done(r1.at[h], ssem.at[h, 0])
+                    out, at = (wide_out, D * part) if part < 3 else (narrow_out, 0)
+                    for j in range(3):
+                        start = at + HALF * t + 128 * j
+                        out[:, start : start + 128] = block[j, :24]
+
+    def sum_sent(h, t):
+        done(r1.at[h, t], ssem.at[h, t, 0])
         for j in range(3):
-            done(r2.at[h, j], ssem.at[h, 1 + j])
-            done(r3.at[h, j], ssem.at[h, 4 + j])
-            done(r4.at[h, j], ssem.at[h, 7 + j])
-        done(r5.at[h], ssem.at[h, 10])
-        done(f.at[h], ssem.at[h, 11])
-
-    def write_grad(h, left, right, part):
+            done(r2.at[h, t, j], ssem.at[h, t, 1 + j])
+            done(r3.at[h, t, j], ssem.at[h, t, 4 + j])
+            done(r4.at[h, t, j], ssem.at[h, t, 7 + j])
+        done(r5.at[h, t], ssem.at[h, t, 10])
+        done(f.at[h, t], ssem.at[h, t, 11])
+
+    def write_grad(h, t, left, left_out, d_out):
+        right = jnp.concatenate([dqkv[:, D * part + HALF * t : D * part + HALF * t + HALF] for part in range(3)], axis=1)
+        right_out = d_out[:, HALF * t : HALF * t + HALF]
+
         def body(zp, _):
-            block = mm(left[pl.ds(pl.multiple_of(192 * zp, 16), 192), :], right)
-            for i in range(8):
-                xp, cp = i // 2, i % 2
-                own_rows = block[24 * i : 24 * i + 24]
-                own_rows = jnp.concatenate([own_rows[:, : D // 2], own_rows[:, D // 2 :]], axis=0).astype(BF16)
-                G[h, cp, 0, xp, part, zp] = own_rows[0:16]
-                G[h, cp, 1, part, zp, xp] = own_rows[16:32]
-                G[h, cp, 2, zp, xp, part] = own_rows[32:48]
+            rows = pl.ds(pl.multiple_of(384 * zp, 128), 384)
+            three = mm(left[rows, :], right)
+            parts = [three[:, HALF * part : HALF * part + HALF] for part in range(3)] + [mm(left_out[rows, :], right_out)]
+
+            def piece(part, z2, xp, cp, j):
+                start = z2 * 192 + (xp * 2 + cp) * 24
+                return parts[part][start : start + 24, 128 * j : 128 * j + 128]
+
+            for j, order in enumerate(ORDERS[h][t]):
+                last = order[2]
+                spans = {"x": 4, "y": 4, "z": 2}
+                spans[last] //= 2
+                for xi, yi, zi, cp in itertools.product(*(range(spans[axis]) for axis in "xyz"), range(2)):
+                    pair = []
+                    for odd in range(2):
+                        xp, part, z2 = xi, yi, zi
+                        if last == "x":
+                            xp = 2 * xi + odd
+                        elif last == "y":
+                            part = 2 * yi + odd
+                        else:
+                            z2 = odd
+                        pair.append(piece(part, z2, xp, cp, j))
+                    at = {"x": xi, "y": yi, "z": zp if last == "z" else 2 * zp + zi}
+                    G[h, t, cp, j, at[order[0]], at[order[1]], at[last]] = jnp.concatenate(pair, axis=0).astype(BF16)
             return 0
 
-        lax.fori_loop(0, 4, body, 0)
+        lax.fori_loop(0, 2, body, 0)
 
     left_half = lax.broadcasted_iota(jnp.int32, (1, 128), 1) < HD
 
@@ -255,7 +289,7 @@
                 att[rows, columns(pair, 0)] = total.astype(BF16)
             return 0
 
-        lax.fori_loop(0, PAIRS, body, 0)
+        lax.fori_loop(0, PAIRS, body, 0, unroll=True)
 
     def attend_back(qkv, probs, size, first, last):
         def body(pair, _):
@@ -280,7 +314,7 @@
                 dqkv[rows, columns(pair, 2)] = d_values.astype(BF16)
             return 0
 
-        lax.fori_loop(first, last, body, 0)
+        lax.fori_loop(first, last, body, 0, unroll=True)
 
     def project(normed, weights, qkv):
         for part in range(3):
@@ -297,17 +331,20 @@
     loads[0].wait()
     rows_in = vid_v[...].astype(F32)
     normed = normalize(rows_in)[0].astype(BF16)
-    loads[1].wait()
-    project(normed, wqs_v, qkv_s)
-    nTs[...] = normed.T
     loads[3].wait()
     sbuf[0] = pack(gout_v[...].astype(F32))
     pl.semaphore_wait(barrier, GROUP - 1 + 7)
-    exchange(0)
+    exchange(0, 1, 20)
+    loads[1].wait()
+    loads[4].start()
+    loads[5].start()
+    project(normed, wqs_v, qkv_s)
+    nTs[...] = normed.T
     attend(qkv_s, probs_s, att_s, ROWS, None)
     loads[2].wait()
     sbuf[1] = pack(vid_v[...].astype(F32) + mm(att_s[...], wos_v[...]))
     exchange(1)
+    exchange(0, 20, GROUP)
 
     r = lax.broadcasted_iota(jnp.int32, (ROWS, ROWS), 0)
     q = lax.broadcasted_iota(jnp.int32, (ROWS, ROWS), 1)
@@ -331,56 +368,83 @@
         == lax.broadcasted_iota(jnp.int32, (128, 128), 1) // 32
     )
     attend(qkv_t, probs_t, att_t, 128, same)
-    low = (tin[...].astype(F32) + mm(att_t[...], wot_v[...])).astype(BF16)
-    sbuf[2] = pack(mm(permT[...], low))
-    exchange(2)
     attend_back(qkv_t, probs_t, 128, 0, PAIRS)
     d_rows = normalize_back(tin[...].astype(F32), project_back(wqt_v))
     low = (gt[...].astype(F32) + d_rows).astype(BF16)
     sbuf[3] = pack(mm(permT[...], low))
     exchange(3)
     aT[...] = att_t[...].T
-    for part in range(3):
-        write_grad(TIME, nT, dqkv[:, part * D : part * D + D], part)
-    write_grad(TIME, aT, gt[...], 3)
-    sum_core_start(TIME)
+    for t in range(2):
+        write_grad(TIME, t, nT, aT, gt)
+        sum_core_start(TIME, t)
+    low = (tin[...].astype(F32) + mm(att_t[...], wot_v[...])).astype(BF16)
+    sbuf[2] = pack(mm(permT[...], low))
+    for t in range(2):
+        sum_add(TIME, t)
+        sum_first(TIME, t)
+    arrived(3)
+    exchange(2)
+
+    d_space[...] = unpack(rbuf[3]).astype(BF16)
+    datt[...] = mm_nt(d_space[...], wos_v[...]).astype(BF16)
+    attend_back(qkv_s, probs_s, ROWS, 0, 3)
+    write_grad(SPACE, 0, nTs, aTs, d_space)
+    sum_core_start(SPACE, 0)
+    attend_back(qkv_s, probs_s, ROWS, 3, 6)
+    sum_add(SPACE, 0)
+    sum_first(SPACE, 0)
+    write_grad(SPACE, 1, nTs, aTs, d_space)
+    sum_core_start(SPACE, 1)
+    d_rows = normalize_back(vid_v[...].astype(F32), project_back(wqs_v))
+    gradv[...] = (d_space[...].astype(F32) + d_rows).astype(BF16)
+    grad_copy = pltpu.make_async_copy(gradv, grad_video, lsem.at[7])
+    grad_copy.start()
+    sum_add(SPACE, 1)
+    sum_first(SPACE, 1)
+    sum_second(TIME, 0)
+    sum_second(TIME, 1)
     arrived(2)
     outv[...] = unpack(rbuf[2]).astype(BF16)
     out_copy = pltpu.make_async_copy(outv, out_video, lsem.at[6])
     out_copy.start()
-    arrived(3)
-
-    d_space = unpack(rbuf[3]).astype(BF16)
-    datt[...] = mm_nt(d_space, wos_v[...]).astype(BF16)
-    write_grad(SPACE, aTs, d_space, 3)
-    attend_back(qkv_s, probs_s, ROWS, 0, 2)
-    sum_first(TIME)
-    attend_back(qkv_s, probs_s, ROWS, 2, 4)
-    sum_second(TIME)
-    attend_back(qkv_s, probs_s, ROWS, 4, 6)
-    sum_third(TIME)
-    for part in range(3):
-        write_grad(SPACE, nTs, dqkv[:, part * D : part * D + D], part)
-    sum_core_start(SPACE)
-    sum_far(TIME)
-    d_rows = normalize_back(vid_v[...].astype(F32), project_back(wqs_v))
-    gradv[...] = (unpack(rbuf[3]) + d_rows).astype(BF16)
-    grad_copy = pltpu.make_async_copy(gradv, grad_video, lsem.at[7])
-    grad_copy.start()
-    sum_gather(TIME)
-    sum_first(SPACE)
-    sum_finish(TIME, oqt, oot)
-    sum_second(SPACE)
-    sum_third(SPACE)
-    sum_far(SPACE)
-    sum_gather(SPACE)
-    sum_finish(SPACE, oqs, oos)
+    sum_second(SPACE, 0)
+    sum_third(TIME, 0)
+    sum_third(TIME, 1)
+    sum_second(SPACE, 1)
+    sum_third(SPACE, 0)
+    sum_far(TIME, 0)
+    sum_far(TIME, 1)
+    sum_third(SPACE, 1)
+    sum_far(SPACE, 0)
+    sum_gather(TIME, 0)
+    sum_gather(TIME, 1)
+    sum_far(SPACE, 1)
+    sum_gather(SPACE, 0)
+    sum_finish(TIME, 0, oqt, oot)
+    sum_finish(TIME, 1, oqt, oot)
+    sum_gather(SPACE, 1)
+    sum_finish(SPACE, 0, oqs, oos)
+    sum_finish(SPACE, 1, oqs, oos)
     for i in range(4):
         done(rbuf.at[i, pl.ds(0, GROUP - 1)], asem.at[i])
-    sum_sent(TIME)
-    sum_sent(SPACE)
+    for t in range(2):
+        sum_sent(TIME, t)
+        sum_sent(SPACE, t)
     out_copy.wait()
     grad_copy.wait()
+
+
+def hand_over(*refs):
+    sources, targets, held, sems = refs[:6], refs[6:12], refs[12:18], refs[18]
+    loads = [pltpu.make_async_copy(sources[i], held[i], sems.at[0, i]) for i in range(6)]
+    stores = [pltpu.make_async_copy(held[i], targets[i], sems.at[1, i]) for i in range(6)]
+    for load in loads:
+        load.start()
+    for load, store in zip(loads, stores):
+        load.wait()
+        store.start()
+    for store in stores:
+        store.wait()
 
 
 def shards(video, w_qkv_space, w_out_space, w_qkv_time, w_out_time, grad_out):
@@ -399,13 +463,13 @@
             V(ROWS, D), V(ROWS, D), V(D, 3 * D), V(D, D), V(D, 3 * D), V(D, D),
             V(ROWS, 3 * D), V(ROWS, 3 * D), V(ROWS, D), V(ROWS, D), V(ROWS, 3 * D), V(ROWS, D),
             V(ROWS, D), V(ROWS, D), V(D, ROWS), V(D, ROWS), V(D, ROWS), V(D, ROWS),
-            V(12, ROWS, ROWS), V(12, ROWS, 128), V(ROWS, ROWS), V(ROWS, ROWS), V(ROWS, D), V(ROWS, D),
+            V(12, ROWS, ROWS), V(12, ROWS, 128), V(ROWS, ROWS), V(ROWS, ROWS), V(ROWS, D), V(ROWS, D), V(ROWS, D),
             V(4, GROUP, 16, 384), V(4, GROUP, 16, 384),
-            V(2, 2, 3, 4, 4, 4, 16, 384), V(2, 3, 4, 4, 4, 16, 384), V(2, 3, 3, 4, 4, 16, 384),
-            V(2, 3, 4, 4, 16, 384), V(2, 3, 3, 4, 16, 384), V(2, 3, 4, 16, 384), V(2, 3, 3, 16, 384),
-            V(2, 3, 16, 384), V(2, 3, 16, 384), V(2, 3, 16, 384), V(2, 3, 3, 16, 384),
+            V(2, 2, 2, 3, 4, 4, 2, 48, 128), V(2, 2, 3, 4, 4, 2, 48, 128), V(2, 2, 3, 3, 4, 2, 48, 128),
+            V(2, 2, 3, 4, 2, 48, 128), V(2, 2, 3, 3, 2, 48, 128), V(2, 2, 3, 4, 32, 128), V(2, 2, 3, 3, 32, 128),
+            V(2, 2, 3, 32, 128), V(2, 2, 3, 32, 128), V(2, 2, 3, 32, 128), V(2, 2, 3, 3, 32, 128),
             pltpu.SemaphoreType.DMA((8,)), pltpu.SemaphoreType.DMA((4,)), pltpu.SemaphoreType.DMA((4,)),
-            pltpu.SemaphoreType.DMA((2, 12)), pltpu.SemaphoreType.DMA((2, 12)),
+            pltpu.SemaphoreType.DMA((2, 2, 12)), pltpu.SemaphoreType.DMA((2, 2, 12)),
         ],
         compiler_params=pltpu.CompilerParams(
             collective_id=0, has_side_effects=True, vmem_limit_bytes=60 * 2**20
@@ -414,6 +478,14 @@
     )(
         video.reshape(ROWS, D), w_qkv_space, w_out_space, w_qkv_time, w_out_time, grad_out.reshape(ROWS, D)
     )
+    outs = pl.pallas_call(
+        hand_over,
+        out_shape=[jax.ShapeDtypeStruct(o.shape, o.dtype) for o in outs],
+        in_specs=[anywhere] * 6,
+        out_specs=[anywhere] * 6,
+        scratch_shapes=[pltpu.VMEM(o.shape, o.dtype) for o in outs] + [pltpu.SemaphoreType.DMA((2, 6))],
+        name="hand_over",
+    )(*outs)
     shape = (1, 1, ROWS, D)
     return (outs[0].reshape(shape), outs[1].reshape(shape), outs[2], outs[3], outs[4], outs[5])
 

time: 126 us -> 98.9 us (0.78)
  Pallas kernels: 115 us -> 98 us
  local copies, waits for them, and re-layouts: 9.84 us -> 0 us
    pallas_call x1, Pallas kernels: 115 us -> 95.8 us  [shards(): pl.pallas_call(kernel, out_shape=[tokens, tokens, wide, narrow, wide, nar...]
    unnamed x6 -> x0, local copies, waits for them, and re-layouts: 9.84 us -> none
    pallas_call x0 -> x1, Pallas kernels: none -> 2.16 us  [shards(): pl.pallas_call(hand_over, out_shape=[jax.ShapeDtypeStruct(o.shape, o.dtyp...]
where the time goes in v2:
time: 98.9 us; the launch traced here: 98.8 us
  Pallas kernels  98 us (99%)
    pallas_call x1, Pallas kernels, shards(): pl.pallas_call(kernel, out_shape=[tokens, tokens, wide, narrow, wide, nar...  95.8 us
    pallas_call x1, Pallas kernels, shards(): pl.pallas_call(hand_over, out_shape=[jax.ShapeDtypeStruct(o.shape, o.dtyp...  2.16 us

profile of v2, /device:TPU:8, one launch (start us, length us, event | category | flops | bytes accessed | tf_op | source)
XLA Modules:
  0.0 98.8 jit_solution(8526211395510878026)
XLA Ops:
  0.6 95.8 %layer.1 = (bf16[256,768]{1,0:T(8,128)(2,1)}, bf16[256,768]{1,0:T(8,128)(2,1)}, f32[24,2304]{1,0:T(8,128)}, f32[24,768]{1,0:T(8,128)}, f32[24,2304]{1,0:T(8,128)}, /*index=5*/f32[24,768]{1,0:T(8,128)}) custom-call(bf16[256,768]{1,0:T(8,128)(2,1)} %bitcast.4, bf16[768,2304]{1,0:T(8,128)(2,1)} %wqs.1, bf16[768,768]{1,0:T(8,128)(2,1)} %wos.1, ...), custom_call_target="tpu_custom_call" | custom-call | tf_op jit(solution)/shard_map/layer/pallas_call | solution.py:457
  96.5 2.2 %hand_over.1 = (bf16[256,768]{1,0:T(8,128)(2,1)}, bf16[256,768]{1,0:T(8,128)(2,1)}, f32[24,2304]{1,0:T(8,128)}, f32[24,768]{1,0:T(8,128)}, f32[24,2304]{1,0:T(8,128)}, /*index=5*/f32[24,768]{1,0:T(8,128)}) custom-call(bf16[256,768]{1,0:T(8,128)(2,1)} %get-tuple-element.18.refs_0_, bf16[256,768]{1,0:T(8,128)(2,1)} %get-tuple-element.19.refs_1_, ...), custom_call_target="tpu_custom_call" | custom-call | tf_op jit(solution)/shard_map/hand_over/pallas_call | solution.py:481

commit v3 on v2

--- a/solution.py
+++ b/solution.py
@@ -79,7 +79,7 @@
     out_video, grad_video, oqs, oos, oqt, oot,
     vid_v, gout_v, wqs_v, wos_v, wqt_v, wot_v,
     qkv_s, qkv_t, att_s, att_t, dqkv, datt, tin, gt, nT, aT, nTs, aTs,
-    probs_s, probs_t, perm, permT, outv, gradv, d_space,
+    probs_s, probs_t, bias, outv, gradv, d_space,
     sbuf, rbuf, G, r1, r2, b, r3, cc, r4, d, r5, e, f,
     lsem, asem, arsem, ssem, rsem,
 ):
@@ -136,6 +136,9 @@
         if first == 1:
             rbuf[i, seq] = sbuf[i, seq]
 
+    def left(i):
+        done(rbuf.at[i, pl.ds(0, GROUP - 1)], asem.at[i])
+
     def arrived(i):
         done(rbuf.at[i, pl.ds(0, GROUP - 1)], arsem.at[i])
 
@@ -270,48 +273,42 @@
     def columns(pair, part):
         return pl.ds(pl.multiple_of(part * D + pair * 128, 128), 128)
 
-    def attend(qkv, probs, att, size, mask):
+    def attend(qkv, probs, att, apart):
         def body(pair, _):
-            for blk in range(ROWS // size):
-                rows = slice(blk * size, blk * size + size)
-                queries = halves(qkv[rows, columns(pair, 0)])
-                keys = qkv[rows, columns(pair, 1)]
-                values = halves(qkv[rows, columns(pair, 2)])
-                total = None
-                for s in range(2):
-                    scores = mm_nt(queries[s], keys)
-                    if mask is not None:
-                        scores = jnp.where(mask, scores, -1e30)
-                    low = softmax(scores).astype(BF16)
-                    probs[pair * 2 + s, rows] = low
-                    part = mm(low, values[s])
-                    total = part if total is None else total + part
-                att[rows, columns(pair, 0)] = total.astype(BF16)
+            queries = halves(qkv[:, columns(pair, 0)])
+            keys = qkv[:, columns(pair, 1)]
+            values = halves(qkv[:, columns(pair, 2)])
+            total = 0.0
+            for s in range(2):
+                scores = mm_nt(queries[s], keys)
+                if apart is not None:
+                    scores = scores + apart[...]
+                low = softmax(scores).astype(BF16)
+                probs[pair * 2 + s] = low
+                total = total + mm(low, values[s])
+            att[:, columns(pair, 0)] = total.astype(BF16)
             return 0
 
         lax.fori_loop(0, PAIRS, body, 0, unroll=True)
 
-    def attend_back(qkv, probs, size, first, last):
+    def attend_back(qkv, probs, first, last):
         def body(pair, _):
-            for blk in range(ROWS // size):
-                rows = slice(blk * size, blk * size + size)
-                queries = halves(qkv[rows, columns(pair, 0)])
-                keys = halves(qkv[rows, columns(pair, 1)])
-                values = qkv[rows, columns(pair, 2)]
-                d_out = halves(datt[rows, columns(pair, 0)])
-                d_queries = d_keys = d_values = 0.0
-                for s in range(2):
-                    low = probs[pair * 2 + s, rows]
-                    wide = low.astype(F32)
-                    d_probs = mm_nt(d_out[s], values)
-                    product = d_probs * wide
-                    d_scores = (product - wide * jnp.sum(product, axis=-1, keepdims=True)).astype(BF16)
-                    d_values = d_values + mm_tn(low, d_out[s])
-                    d_queries = d_queries + mm(d_scores, keys[s])
-                    d_keys = d_keys + mm_tn(d_scores, queries[s])
-                dqkv[rows, columns(pair, 0)] = (d_queries * SCALE).astype(BF16)
-                dqkv[rows, columns(pair, 1)] = (d_keys * SCALE).astype(BF16)
-                dqkv[rows, columns(pair, 2)] = d_values.astype(BF16)
+            queries = halves(qkv[:, columns(pair, 0)])
+            keys = halves(qkv[:, columns(pair, 1)])
+            values = qkv[:, columns(pair, 2)]
+            d_out = halves(datt[:, columns(pair, 0)])
+            d_queries = d_keys = d_values = 0.0
+            for s in range(2):
+                low = probs[pair * 2 + s]
+                wide = low.astype(F32)
+                product = mm_nt(d_out[s], values) * wide
+                d_scores = (product - wide * jnp.sum(product, axis=-1, keepdims=True)).astype(BF16)
+                d_values = d_values + mm_tn(low, d_out[s])
+                d_queries = d_queries + mm(d_scores, keys[s])
+                d_keys = d_keys + mm_tn(d_scores, queries[s])
+            dqkv[:, columns(pair, 0)] = (d_queries * SCALE).astype(BF16)
+            dqkv[:, columns(pair, 1)] = (d_keys * SCALE).astype(BF16)
+            dqkv[:, columns(pair, 2)] = d_values.astype(BF16)
             return 0
 
         lax.fori_loop(first, last, body, 0, unroll=True)
@@ -329,56 +326,47 @@
         return total
 
     loads[0].wait()
-    rows_in = vid_v[...].astype(F32)
-    normed = normalize(rows_in)[0].astype(BF16)
-    loads[3].wait()
-    sbuf[0] = pack(gout_v[...].astype(F32))
-    pl.semaphore_wait(barrier, GROUP - 1 + 7)
-    exchange(0, 1, 20)
+    normed = normalize(vid_v[...].astype(F32))[0].astype(BF16)
     loads[1].wait()
     loads[4].start()
     loads[5].start()
     project(normed, wqs_v, qkv_s)
-    nTs[...] = normed.T
-    attend(qkv_s, probs_s, att_s, ROWS, None)
+    attend(qkv_s, probs_s, att_s, None)
     loads[2].wait()
     sbuf[1] = pack(vid_v[...].astype(F32) + mm(att_s[...], wos_v[...]))
+    pl.semaphore_wait(barrier, GROUP - 1 + 7)
     exchange(1)
-    exchange(0, 20, GROUP)
-
-    r = lax.broadcasted_iota(jnp.int32, (ROWS, ROWS), 0)
-    q = lax.broadcasted_iota(jnp.int32, (ROWS, ROWS), 1)
-    perm[...] = jnp.where(q == (r % 32) * 8 + r // 32, 1.0, 0.0).astype(BF16)
-    permT[...] = jnp.where(r == (q % 32) * 8 + q // 32, 1.0, 0.0).astype(BF16)
+    loads[3].wait()
+    sbuf[0] = pack(gout_v[...].astype(F32))
+
+    ahead = lax.broadcasted_iota(jnp.int32, (ROWS, ROWS), 0) + (ROWS - lax.broadcasted_iota(jnp.int32, (ROWS, ROWS), 1))
+    bias[...] = jnp.where(ahead % 8 == 0, 0.0, -1e30)
+    nTs[...] = normalize(vid_v[...].astype(F32))[0].astype(BF16).T
     aTs[...] = att_s[...].T
-    arrived(0)
-    gt[...] = mm(perm[...], unpack(rbuf[0]).astype(BF16)).astype(BF16)
     loads[4].wait()
     loads[5].wait()
-    datt[...] = mm_nt(gt[...], wot_v[...]).astype(BF16)
+    left(1)
+    exchange(0)
     arrived(1)
 
-    rows_in = mm(perm[...], unpack(rbuf[1]).astype(BF16))
+    rows_in = unpack(rbuf[1])
     tin[...] = rows_in.astype(BF16)
     normed = normalize(rows_in)[0].astype(BF16)
     project(normed, wqt_v, qkv_t)
+    attend(qkv_t, probs_t, att_t, bias)
     nT[...] = normed.T
-    same = (
-        lax.broadcasted_iota(jnp.int32, (128, 128), 0) // 32
-        == lax.broadcasted_iota(jnp.int32, (128, 128), 1) // 32
-    )
-    attend(qkv_t, probs_t, att_t, 128, same)
-    attend_back(qkv_t, probs_t, 128, 0, PAIRS)
+    aT[...] = att_t[...].T
+    sbuf[2] = pack(tin[...].astype(F32) + mm(att_t[...], wot_v[...]))
+    arrived(0)
+    gt[...] = unpack(rbuf[0]).astype(BF16)
+    datt[...] = mm_nt(gt[...], wot_v[...]).astype(BF16)
+    attend_back(qkv_t, probs_t, 0, PAIRS)
     d_rows = normalize_back(tin[...].astype(F32), project_back(wqt_v))
-    low = (gt[...].astype(F32) + d_rows).astype(BF16)
-    sbuf[3] = pack(mm(permT[...], low))
+    sbuf[3] = pack(gt[...].astype(F32) + d_rows)
     exchange(3)
-    aT[...] = att_t[...].T
     for t in range(2):
         write_grad(TIME, t, nT, aT, gt)
         sum_core_start(TIME, t)
-    low = (tin[...].astype(F32) + mm(att_t[...], wot_v[...])).astype(BF16)
-    sbuf[2] = pack(mm(permT[...], low))
     for t in range(2):
         sum_add(TIME, t)
         sum_first(TIME, t)
@@ -387,14 +375,14 @@
 
     d_space[...] = unpack(rbuf[3]).astype(BF16)
     datt[...] = mm_nt(d_space[...], wos_v[...]).astype(BF16)
-    attend_back(qkv_s, probs_s, ROWS, 0, 3)
+    attend_back(qkv_s, probs_s, 0, 3)
     write_grad(SPACE, 0, nTs, aTs, d_space)
     sum_core_start(SPACE, 0)
-    attend_back(qkv_s, probs_s, ROWS, 3, 6)
+    attend_back(qkv_s, probs_s, 3, 6)
+    write_grad(SPACE, 1, nTs, aTs, d_space)
+    sum_core_start(SPACE, 1)
     sum_add(SPACE, 0)
     sum_first(SPACE, 0)
-    write_grad(SPACE, 1, nTs, aTs, d_space)
-    sum_core_start(SPACE, 1)
     d_rows = normalize_back(vid_v[...].astype(F32), project_back(wqs_v))
     gradv[...] = (d_space[...].astype(F32) + d_rows).astype(BF16)
     grad_copy = pltpu.make_async_copy(gradv, grad_video, lsem.at[7])
@@ -425,8 +413,8 @@
     sum_gather(SPACE, 1)
     sum_finish(SPACE, 0, oqs, oos)
     sum_finish(SPACE, 1, oqs, oos)
-    for i in range(4):
-        done(rbuf.at[i, pl.ds(0, GROUP - 1)], asem.at[i])
+    for i in (0, 2, 3):
+        left(i)
     for t in range(2):
         sum_sent(TIME, t)
         sum_sent(SPACE, t)
@@ -463,7 +451,7 @@
             V(ROWS, D), V(ROWS, D), V(D, 3 * D), V(D, D), V(D, 3 * D), V(D, D),
             V(ROWS, 3 * D), V(ROWS, 3 * D), V(ROWS, D), V(ROWS, D), V(ROWS, 3 * D), V(ROWS, D),
             V(ROWS, D), V(ROWS, D), V(D, ROWS), V(D, ROWS), V(D, ROWS), V(D, ROWS),
-            V(12, ROWS, ROWS), V(12, ROWS, 128), V(ROWS, ROWS), V(ROWS, ROWS), V(ROWS, D), V(ROWS, D), V(ROWS, D),
+            V(12, ROWS, ROWS), V(12, ROWS, ROWS), pltpu.VMEM((ROWS, ROWS), F32), V(ROWS, D), V(ROWS, D), V(ROWS, D),
             V(4, GROUP, 16, 384), V(4, GROUP, 16, 384),
             V(2, 2, 2, 3, 4, 4, 2, 48, 128), V(2, 2, 3, 4, 4, 2, 48, 128), V(2, 2, 3, 3, 4, 2, 48, 128),
             V(2, 2, 3, 4, 2, 48, 128), V(2, 2, 3, 3, 2, 48, 128), V(2, 2, 3, 4, 32, 128), V(2, 2, 3, 3, 32, 128),

time: 98.9 us -> 94.9 us (0.960)
  Pallas kernels: 98 us -> 93.4 us
    pallas_call x1, Pallas kernels: 95.8 us -> 91.3 us  [shards(): pl.pallas_call(kernel, out_shape=[tokens, tokens, wide, narrow, wide, nar...]
where the time goes in v3:
time: 94.9 us; the launch traced here: 94.2 us
  Pallas kernels  93.4 us (98%)
    pallas_call x1, Pallas kernels, shards(): pl.pallas_call(kernel, out_shape=[tokens, tokens, wide, narrow, wide, nar...  91.3 us
    pallas_call x1, Pallas kernels, shards(): pl.pallas_call(hand_over, out_shape=[jax.ShapeDtypeStruct(o.shape, o.dtyp...  2.16 us

profile of v3, /device:TPU:8, one launch (start us, length us, event | category | flops | bytes accessed | tf_op | source)
XLA Modules:
  0.0 94.2 jit_solution(17540857984979801544)
XLA Ops:
  0.6 91.3 %layer.1 = (bf16[256,768]{1,0:T(8,128)(2,1)}, bf16[256,768]{1,0:T(8,128)(2,1)}, f32[24,2304]{1,0:T(8,128)}, f32[24,768]{1,0:T(8,128)}, f32[24,2304]{1,0:T(8,128)}, /*index=5*/f32[24,768]{1,0:T(8,128)}) custom-call(bf16[256,768]{1,0:T(8,128)(2,1)} %bitcast.4, bf16[768,2304]{1,0:T(8,128)(2,1)} %wqs.1, bf16[768,768]{1,0:T(8,128)(2,1)} %wos.1, ...), custom_call_target="tpu_custom_call" | custom-call | tf_op jit(solution)/shard_map/layer/pallas_call | solution.py:445
  91.9 2.2 %hand_over.1 = (bf16[256,768]{1,0:T(8,128)(2,1)}, bf16[256,768]{1,0:T(8,128)(2,1)}, f32[24,2304]{1,0:T(8,128)}, f32[24,768]{1,0:T(8,128)}, f32[24,2304]{1,0:T(8,128)}, /*index=5*/f32[24,768]{1,0:T(8,128)}) custom-call(bf16[256,768]{1,0:T(8,128)(2,1)} %get-tuple-element.18.refs_0_, bf16[256,768]{1,0:T(8,128)(2,1)} %get-tuple-element.19.refs_1_, ...), custom_call_target="tpu_custom_call" | custom-call | tf_op jit(solution)/shard_map/hand_over/pallas_call | solution.py:469

commit v4 on v3

--- a/solution.py
+++ b/solution.py
@@ -22,7 +22,7 @@
 SCALE_LOG2E = SCALE * math.log2(math.e)
 TIME, SPACE = 0, 1
 ORDERS = (
-    (("xyz", "yzx", "xzy"), ("xyz", "yzx", "yxz")),
+    (("xyz", "yzx", "yxz"), ("xyz", "yzx", "zxy")),
     (("xyz", "yzx", "zxy"), ("xyz", "yzx", "zxy")),
 )
 
@@ -369,8 +369,9 @@
         sum_core_start(TIME, t)
     for t in range(2):
         sum_add(TIME, t)
-        sum_first(TIME, t)
+        sum_first(TIME, t, (0, 1, 2)[: 3 - t])
     arrived(3)
+    sum_first(TIME, 1, (2,))
     exchange(2)
 
     d_space[...] = unpack(rbuf[3]).astype(BF16)
@@ -389,29 +390,29 @@
     grad_copy.start()
     sum_add(SPACE, 1)
     sum_first(SPACE, 1)
-    sum_second(TIME, 0)
-    sum_second(TIME, 1)
     arrived(2)
     outv[...] = unpack(rbuf[2]).astype(BF16)
     out_copy = pltpu.make_async_copy(outv, out_video, lsem.at[6])
     out_copy.start()
     sum_second(SPACE, 0)
+    sum_second(TIME, 0)
+    sum_second(TIME, 1)
+    sum_second(SPACE, 1)
+    sum_third(SPACE, 0)
     sum_third(TIME, 0)
     sum_third(TIME, 1)
-    sum_second(SPACE, 1)
-    sum_third(SPACE, 0)
+    sum_third(SPACE, 1)
+    sum_far(SPACE, 0)
     sum_far(TIME, 0)
     sum_far(TIME, 1)
-    sum_third(SPACE, 1)
-    sum_far(SPACE, 0)
+    sum_far(SPACE, 1)
+    sum_gather(SPACE, 0)
     sum_gather(TIME, 0)
     sum_gather(TIME, 1)
-    sum_far(SPACE, 1)
-    sum_gather(SPACE, 0)
+    sum_gather(SPACE, 1)
+    sum_finish(SPACE, 0, oqs, oos)
     sum_finish(TIME, 0, oqt, oot)
     sum_finish(TIME, 1, oqt, oot)
-    sum_gather(SPACE, 1)
-    sum_finish(SPACE, 0, oqs, oos)
     sum_finish(SPACE, 1, oqs, oos)
     for i in (0, 2, 3):
         left(i)

time: 94.9 us -> 92.7 us (0.977)
  Pallas kernels: 93.4 us -> 90.8 us
    pallas_call x1, Pallas kernels: 91.3 us -> 88.6 us  [shards(): pl.pallas_call(kernel, out_shape=[tokens, tokens, wide, narrow, wide, nar...]
where the time goes in v4:
time: 92.7 us; the launch traced here: 91.6 us
  Pallas kernels  90.8 us (98%)
    pallas_call x1, Pallas kernels, shards(): pl.pallas_call(kernel, out_shape=[tokens, tokens, wide, narrow, wide, nar...  88.6 us
    pallas_call x1, Pallas kernels, shards(): pl.pallas_call(hand_over, out_shape=[jax.ShapeDtypeStruct(o.shape, o.dtyp...  2.16 us

profile of v4, /device:TPU:8, one launch (start us, length us, event | category | flops | bytes accessed | tf_op | source)
XLA Modules:
  0.0 91.6 jit_solution(6545024500990026795)
XLA Ops:
  0.6 88.6 %layer.1 = (bf16[256,768]{1,0:T(8,128)(2,1)}, bf16[256,768]{1,0:T(8,128)(2,1)}, f32[24,2304]{1,0:T(8,128)}, f32[24,768]{1,0:T(8,128)}, f32[24,2304]{1,0:T(8,128)}, /*index=5*/f32[24,768]{1,0:T(8,128)}) custom-call(bf16[256,768]{1,0:T(8,128)(2,1)} %bitcast.4, bf16[768,2304]{1,0:T(8,128)(2,1)} %wqs.1, bf16[768,768]{1,0:T(8,128)(2,1)} %wos.1, ...), custom_call_target="tpu_custom_call" | custom-call | tf_op jit(solution)/shard_map/layer/pallas_call | solution.py:446
  89.3 2.2 %hand_over.1 = (bf16[256,768]{1,0:T(8,128)(2,1)}, bf16[256,768]{1,0:T(8,128)(2,1)}, f32[24,2304]{1,0:T(8,128)}, f32[24,768]{1,0:T(8,128)}, f32[24,2304]{1,0:T(8,128)}, /*index=5*/f32[24,768]{1,0:T(8,128)}) custom-call(bf16[256,768]{1,0:T(8,128)(2,1)} %get-tuple-element.18.refs_0_, bf16[256,768]{1,0:T(8,128)(2,1)} %get-tuple-element.19.refs_1_, ...), custom_call_target="tpu_custom_call" | custom-call | tf_op jit(solution)/shard_map/hand_over/pallas_call | solution.py:470
